TPU v7x, 32 devices: a whole 2x2x4 slice. The times are simulated.
32 devices in a mesh: wide: 8 (over z, y), narrow: 4 (over x, core).
Axes of the slice: x: 2, y: 2, z: 4, core: 2. Of those that a mesh axis runs over, the one named last changes fastest.
Arguments:
- matrix: float32 [65536, 1024], P(('wide', 'narrow')), may hold values from -0.078125 to 0.078125
- hashes: int32 [65536], P(('wide', 'narrow')), may hold values from 0 to 2047
- sign_bits: int32 [65536], P(('wide', 'narrow')), may hold values from 0 to 1
- targets: float32 [8, 65536], P(None, ('wide', 'narrow')), may hold values from -6 to 6
Outputs:
- r_factor: float32 [1024, 1024], P('narrow')
- projected: float32 [8, 1024], replicated
- estimate: float32 [8, 1024], replicated
All inputs are finite; a program needn't handle non-finite values.
Results may differ from a plain program's by a relative error of at most 0.0003.
Values sent between devices are 32-bit elements; how exact they have to be, the bound alone decides.
No kernel may reach another device: no remote copies, remote signals or barrier semaphores. Data moves between devices by JAX's collectives and lax.ppermute only.
A program may use at most 128 MiB of HBM per device.

v0:
```python
import jax
import jax.numpy as jnp
from jax import lax
from jax.sharding import PartitionSpec as P

S = 2048


def product(left, right):
    return jnp.dot(left, right, precision=lax.Precision.HIGHEST, preferred_element_type=jnp.float32)


def factor_block(block_matrix):
    size = block_matrix.shape[0]
    places = lax.iota(jnp.int32, size)

    def column_step(step_index, state_pair):
        remaining, lower_part = state_pair
        column = lax.dynamic_slice_in_dim(remaining, step_index, 1, 1)[:, 0]
        pivot_value = jnp.sqrt(lax.dynamic_slice_in_dim(column, step_index, 1, 0)[0])
        scaled = jnp.where(places >= step_index, column / pivot_value, 0.0)
        lower_part = lax.dynamic_update_slice_in_dim(lower_part, scaled[:, None], step_index, 1)
        remaining = remaining - scaled[:, None] * scaled[None, :]
        return (remaining, lower_part)

    final_pair = lax.fori_loop(0, size, column_step, (block_matrix, jnp.zeros_like(block_matrix)))
    return final_pair[1]


def invert_lower(lower_part):
    size = lower_part.shape[0]
    diag_values = jnp.diagonal(lower_part)
    unit_part = lower_part / diag_values[:, None]
    eye_matrix = jnp.eye(size, dtype=jnp.float32)
    strict_part = eye_matrix - unit_part
    inverse = eye_matrix + strict_part
    power = strict_part
    rounds = max(0, (size - 1).bit_length() - 1)
    for round_index in range(rounds):
        power = product(power, power)
        inverse = product(inverse, eye_matrix + power)
    return inverse / diag_values[None, :]


def blocked_cholesky(gram_matrix):
    width = gram_matrix.shape[0]
    block_size = min(128, width)
    block_count = width // block_size
    remaining = gram_matrix
    panels = []
    inverses = []
    for block_index in range(block_count):
        first = block_index * block_size
        after = first + block_size
        diag_block = remaining[first:after, first:after]
        diag_lower = factor_block(diag_block)
        diag_inverse = invert_lower(diag_lower)
        inverses.append(diag_inverse)
        below = remaining[after:, first:after]
        below_lower = product(below, diag_inverse.T)
        if after < width:
            remaining = remaining.at[after:, after:].add(-product(below_lower, below_lower.T))
        panel = jnp.concatenate(
            [jnp.zeros((first, block_size), jnp.float32), diag_lower, below_lower], axis=0
        )
        panels.append(panel)
    return (jnp.concatenate(panels, axis=1), inverses, block_size)


def forward_solve(lower_factor, inverses, block_size, values):
    pieces = []
    for block_index in range(len(inverses)):
        first = block_index * block_size
        after = first + block_size
        rest = values[first:after]
        if block_index > 0:
            rest = rest - product(
                lower_factor[first:after, :first], jnp.concatenate(pieces, axis=0)
            )
        pieces.append(product(inverses[block_index], rest))
    return jnp.concatenate(pieces, axis=0)


def backward_solve(lower_factor, inverses, block_size, values):
    width = lower_factor.shape[0]
    pieces = []
    for block_index in reversed(range(len(inverses))):
        first = block_index * block_size
        after = first + block_size
        rest = values[first:after]
        if after < width:
            rest = rest - product(
                lower_factor[after:, first:after].T, jnp.concatenate(pieces, axis=0)
            )
        pieces.insert(0, product(inverses[block_index].T, rest))
    return jnp.concatenate(pieces, axis=0)


def shards(matrix, hashes, sign_bits, targets):
    rows_local = matrix.shape[0]
    width = matrix.shape[1]
    row_signs = (2 * sign_bits - 1).astype(jnp.float32)
    block = min(512, rows_local)
    block_count = rows_local // block
    bucket_range = lax.iota(jnp.int32, S)

    def add_block(block_index, running):
        offset = block_index * block
        bucket_ids = lax.dynamic_slice_in_dim(hashes, offset, block, 0)
        block_signs = lax.dynamic_slice_in_dim(row_signs, offset, block, 0)
        block_rows = lax.dynamic_slice_in_dim(matrix, offset, block, 0)
        one_hot = jnp.where(bucket_range[:, None] == bucket_ids[None, :], block_signs[None, :], 0.0)
        return running + jnp.dot(
            one_hot, block_rows, precision=lax.Precision.HIGHEST, preferred_element_type=jnp.float32
        )

    partial_sketch = lax.fori_loop(0, block_count, add_block, jnp.zeros((S, width), jnp.float32))
    moments_local = jnp.dot(
        targets, matrix, precision=lax.Precision.HIGHEST, preferred_element_type=jnp.float32
    )
    owned_rows = lax.psum_scatter(
        partial_sketch, ("wide", "narrow"), scatter_dimension=0, tiled=True
    )
    gram_matrix, moments = lax.psum(
        (
            lax.dot_general(
                owned_rows,
                owned_rows,
                (((0,), (0,)), ((), ())),
                precision=lax.Precision.HIGHEST,
                preferred_element_type=jnp.float32,
            ),
            moments_local,
        ),
        ("wide", "narrow"),
    )
    lower_factor, inverses, block_size = blocked_cholesky(gram_matrix)
    share = width // lax.axis_size("narrow")
    r_rows = lax.dynamic_slice_in_dim(lower_factor.T, lax.axis_index("narrow") * share, share, 0)
    projected_cols = forward_solve(lower_factor, inverses, block_size, moments.T)
    estimate_cols = backward_solve(lower_factor, inverses, block_size, projected_cols)
    return (r_rows, projected_cols.T, estimate_cols.T)


def solution(mesh):
    return jax.shard_map(
        shards,
        mesh=mesh,
        in_specs=(
            P(("wide", "narrow"), None),
            P(("wide", "narrow")),
            P(("wide", "narrow")),
            P(None, ("wide", "narrow")),
        ),
        out_specs=(P("narrow", None), P(), P()),
        check_vma=False,
    )
```

profile of v0, /device:TPU:0, one launch (start us, length us, event | category | flops | bytes accessed | tf_op | source)
XLA Modules:
  0.0 1943.6 jit_solution(2677816517312669568)
XLA Ops:
  7.2 0.7 add_convert_fusion
  7.9 72.6 %while.181 = (s32[]{:T(128)}, f32[2048,1024]{1,0:T(8,128)}, s32[2048]{0:T(1024)}, f32[2048]{0:T(1024)S(1)}, f32[2048,1024]{1,0:T(8,128)}, /*index=5*/s32[]{:T(128)}, s32[]{:T(128)}, s32[]{:T(128)}, s32[]{:T(128)}) while((s32[]{:T(128)}, f32[2048,1024]{1,0:T(8,128)}, s32[2048]{0:T(1024)}, f32[2048]{0:T(1024)S(1)}, ...), condition=%wide.region_1.2_spmd.clone, body=%wide.region_0.1_spmd.clone.sunk | while | flops 12891193344 | bytes 18886824 | solution.py:117
  8.0 0.8 dynamic_slice.211
  8.8 16.8 select_add_fusion.2
  25.6 0.8 dynamic_slice.211
  26.4 17.5 select_add_fusion.2
  44.0 0.8 dynamic_slice.211
  44.7 17.5 select_add_fusion.2
  62.3 0.8 dynamic_slice.211
  63.1 17.5 select_add_fusion.2
  80.6 151.3 %reduce-scatter.2.cloned.1.call-done = f32[64,1024]{1,0:T(8,128)} async-done(((f32[2048,1024]{1,0:T(8,128)}), f32[64,1024]{1,0:T(8,128)}) %reduce-scatter.2.cloned.1.call-update) | async-done | bytes 262160 | tf_op jit(solution)/shard_map/reduce_scatter | solution.py:121
  231.9 6.5 fusion.178
  238.5 7.3 fusion.207
  245.9 38.0 %psum.15 = f32[1024,8]{0,1:T(8,128)} all-reduce(f32[1024,8]{0,1:T(8,128)S(1)} %fusion.207), channel_id=1, replica_groups=mesh['wide'=8,'narrow'=4] {'wide','narrow'}, use_global_device_ids=true, to_apply=%region_20.21 | all-reduce | flops 8192 | bytes 65536 | tf_op jit(solution)/shard_map/psum | solution.py:124
  283.9 92.9 %all-reduce.3.cloned.1.call-done = f32[1024,1024]{1,0:T(8,128)} async-done(((f32[1024,1024]{1,0:T(8,128)}), f32[1024,1024]{1,0:T(8,128)}) %all-reduce.3.cloned.1.call-update) | async-done | bytes 4194320 | tf_op jit(solution)/shard_map/psum | solution.py:124
  376.8 0.8 slice.325
  377.7 185.7 %while.173 = (s32[]{:T(128)}, f32[128,128]{0,1:T(8,128)S(1)}, f32[128,128]{0,1:T(8,128)S(1)}, s32[]{:T(128)}, s32[]{:T(128)}, /*index=5*/s32[]{:T(128)}) while((s32[]{:T(128)}, f32[128,128]{0,1:T(8,128)S(1)}, f32[128,128]{0,1:T(8,128)S(1)}, s32[]{:T(128)}, s32[]{:T(128)}, /*index=5*/s32[]{:T(128)}) %tuple.452), condition=%wide.region_5.6_spmd.clone, body=%wide.region_4.5_spmd.clone.sunk | while | flops 33411 | bytes 136829 | solution.py:26
  379.2 0.6 dynamic_slice.201
  380.6 0.6 dynamic_slice.201
  383.5 0.6 dynamic_slice.201
  385.0 0.6 dynamic_slice.201
  563.6 1.3 gather_fusion
  567.5 1.6 fusion.42
  569.1 4.8 slice_add_fusion
  574.0 1.6 copy-done.1
  575.7 186.7 %while.174 = (s32[]{:T(128)}, f32[128,128]{0,1:T(8,128)S(1)}, f32[128,128]{0,1:T(8,128)S(1)}, s32[]{:T(128)}, s32[]{:T(128)}, /*index=5*/s32[]{:T(128)}) while((s32[]{:T(128)}, f32[128,128]{0,1:T(8,128)S(1)}, f32[128,128]{0,1:T(8,128)S(1)}, s32[]{:T(128)}, s32[]{:T(128)}, /*index=5*/s32[]{:T(128)}) %tuple.455), condition=%wide.region_7.8_spmd.clone, body=%wide.region_6.7_spmd.clone.sunk | while | flops 33411 | bytes 136829 | solution.py:26
  762.4 1.3 gather_fusion.1
  766.5 1.5 fusion.45
  768.0 2.0 slice_add_fusion.1
  770.1 1.4 copy-done.3
  771.6 186.7 %while.175 = (s32[]{:T(128)}, f32[128,128]{0,1:T(8,128)S(1)}, f32[128,128]{0,1:T(8,128)S(1)}, s32[]{:T(128)}, s32[]{:T(128)}, /*index=5*/s32[]{:T(128)}) while((s32[]{:T(128)}, f32[128,128]{0,1:T(8,128)S(1)}, f32[128,128]{0,1:T(8,128)S(1)}, s32[]{:T(128)}, s32[]{:T(128)}, /*index=5*/s32[]{:T(128)}) %tuple.458), condition=%wide.region_9.10_spmd.clone, body=%wide.region_8.9_spmd.clone.sunk | while | flops 33411 | bytes 136829 | solution.py:26
  958.3 1.5 gather_fusion.2
  962.7 1.4 fusion.52
  964.1 1.4 slice_add_fusion.2
  965.7 186.7 %while.176 = (s32[]{:T(128)}, f32[128,128]{0,1:T(8,128)S(1)}, f32[128,128]{0,1:T(8,128)S(1)}, s32[]{:T(128)}, s32[]{:T(128)}, /*index=5*/s32[]{:T(128)}) while((s32[]{:T(128)}, f32[128,128]{0,1:T(8,128)S(1)}, f32[128,128]{0,1:T(8,128)S(1)}, s32[]{:T(128)}, s32[]{:T(128)}, /*index=5*/s32[]{:T(128)}) %tuple.461), condition=%wide.region_11.12_spmd.clone, body=%wide.region_10.11_spmd.clone.sunk | while | flops 33411 | bytes 136829 | solution.py:26
  1152.5 1.3 gather_fusion.3
  1157.0 1.0 fusion.28
  1158.0 1.0 copy-done.5
  1159.1 186.7 %while.177 = (s32[]{:T(128)}, f32[128,128]{0,1:T(8,128)S(1)}, f32[128,128]{0,1:T(8,128)S(1)}, s32[]{:T(128)}, s32[]{:T(128)}, /*index=5*/s32[]{:T(128)}) while((s32[]{:T(128)}, f32[128,128]{0,1:T(8,128)S(1)}, f32[128,128]{0,1:T(8,128)S(1)}, s32[]{:T(128)}, s32[]{:T(128)}, /*index=5*/s32[]{:T(128)}) %tuple.464), condition=%wide.region_13.14_spmd.clone, body=%wide.region_12.13_spmd.clone.sunk | while | flops 33411 | bytes 136829 | solution.py:26
  1345.8 1.3 gather_fusion.4
  1350.3 0.7 fusion.29
  1351.1 186.7 %while.178 = (s32[]{:T(128)}, f32[128,128]{0,1:T(8,128)S(1)}, f32[128,128]{0,1:T(8,128)S(1)}, s32[]{:T(128)}, s32[]{:T(128)}, /*index=5*/s32[]{:T(128)}) while((s32[]{:T(128)}, f32[128,128]{0,1:T(8,128)S(1)}, f32[128,128]{0,1:T(8,128)S(1)}, s32[]{:T(128)}, s32[]{:T(128)}, /*index=5*/s32[]{:T(128)}) %tuple.467), condition=%wide.region_15.16_spmd.clone, body=%wide.region_14.15_spmd.clone.sunk | while | flops 33411 | bytes 136829 | solution.py:26
  1537.8 1.3 gather_fusion.5
  1542.7 186.7 %while.179 = (s32[]{:T(128)}, f32[128,128]{0,1:T(8,128)S(1)}, f32[128,128]{0,1:T(8,128)S(1)}, s32[]{:T(128)}, s32[]{:T(128)}, /*index=5*/s32[]{:T(128)}) while((s32[]{:T(128)}, f32[128,128]{0,1:T(8,128)S(1)}, f32[128,128]{0,1:T(8,128)S(1)}, s32[]{:T(128)}, s32[]{:T(128)}, /*index=5*/s32[]{:T(128)}) %tuple.470), condition=%wide.region_17.18_spmd.clone, body=%wide.region_16.17_spmd.clone.sunk | while | flops 33411 | bytes 136829 | solution.py:26
  1729.5 1.5 gather_fusion.6
  1734.5 186.7 %while.180 = (s32[]{:T(128)}, f32[128,128]{0,1:T(8,128)S(1)}, f32[128,128]{0,1:T(8,128)S(1)}, s32[]{:T(128)}, s32[]{:T(128)}, /*index=5*/s32[]{:T(128)}) while((s32[]{:T(128)}, f32[128,128]{0,1:T(8,128)S(1)}, f32[128,128]{0,1:T(8,128)S(1)}, s32[]{:T(128)}, s32[]{:T(128)}, /*index=5*/s32[]{:T(128)}) %tuple.473), condition=%wide.region_19.20_spmd.clone, body=%wide.region_18.19_spmd.clone.sunk | while | flops 33411 | bytes 136829 | solution.py:26
  1921.3 1.3 gather_fusion.7
  1935.0 1.3 copy.72
  (5377 shorter events, 778.7 us)
Async XLA Ops:
  7.2 231.4 %copy-start = (f32[8,2048]{1,0:T(8,128)S(1)}, f32[8,2048]{1,0:T(8,128)}, u32[]{:S(2)}) copy-start(f32[8,2048]{1,0:T(8,128)} %param.39) | copy-start | bytes 196612
  7.2 224.7 %reduce-scatter.2.cloned.1.call-start = ((), (), s32[]{:S(2)}) async-start(), calls=%async_computation.1 | async-start | bytes 8650752 | tf_op jit(solution)/shard_map/reduce_scatter | solution.py:121
  80.6 296.2 %all-reduce.3.cloned.1.call-start = ((), (), s32[]{:S(2)}) async-start(), calls=%async_computation.2 | async-start | bytes 8388608 | tf_op jit(solution)/shard_map/psum | solution.py:124
  567.5 6.4 copy-start.19
  574.0 1.6 copy-start.1
  763.8 4.2 copy-start.2
  766.5 5.0 copy-start.15
  770.1 1.4 copy-start.3
  959.9 2.5 copy-start.7
  960.0 4.2 copy-start.4
  962.7 2.9 copy-start.17
  1153.8 2.5 copy-start.9
  1156.6 193.2 %copy-start.11 = (f32[128,128]{1,0:T(8,128)}, f32[128,128]{1,0:T(8,128)S(1)}, u32[]{:S(2)}) copy-start(f32[128,128]{1,0:T(8,128)S(1)} %convolution_divide_fusion.4) | copy-start | bytes 196612
  1158.0 1.0 copy-start.5
  1159.0 191.0 %copy-start.6 = (f32[512,512]{1,0:T(8,128)S(1)}, f32[512,512]{1,0:T(8,128)}, u32[]{:S(2)}) copy-start(f32[512,512]{1,0:T(8,128)} %copy-done.5) | copy-start | bytes 3145732
  1347.2 0.8 copy-start.21
  1350.0 1.0 copy-start.13
  1732.1 191.5 %copy-start.20 = (f32[128,128]{1,0:T(8,128)S(1)}, f32[128,128]{1,0:T(8,128)}, u32[]{:S(2)}) copy-start(f32[128,128]{1,0:T(8,128)} %copy-done.19) | copy-start | bytes 196612
  1732.1 191.5 %copy-start.23 = (f32[1024,8]{0,1:T(8,128)S(1)}, f32[1024,8]{0,1:T(8,128)}, u32[]{:S(2)}) copy-start(f32[1024,8]{0,1:T(8,128)} %psum.15) | copy-start | bytes 98308
  1733.8 192.0 %copy-start.16 = (f32[128,128]{1,0:T(8,128)S(1)}, f32[128,128]{1,0:T(8,128)}, u32[]{:S(2)}) copy-start(f32[128,128]{1,0:T(8,128)} %copy-done.15) | copy-start | bytes 196612
  1921.2 5.0 copy-start.18
  1921.3 5.2 copy-start.8
  1923.4 3.4 copy-start.12
  1923.4 3.6 copy-start.10
  1927.6 0.8 copy-start.14
  1927.7 1.0 copy-start.22
  1931.4 5.0 copy-start.24
  1934.8 1.5 copy-start.25
Sparse Core Ops, SparseCore 0:
  80.7 151.1 reduce-scatter.1
  238.6 138.1 all-reduce.2
where the time goes:
time: 1960 us; the launch traced here: 1940 us
  loops' own time  746 us (38%)
  local copies, waits for them, and re-layouts  667 us (34%)
  waiting for transfers between devices  244 us (12%)
  matrix products  127 us (6%)
  other arithmetic  104 us (5%)
  blocking collectives  38 us (2%)
    another operation x8, loops' own time, factor_block(): lax.fori_loop(0, size, column_step, (block_matrix, jnp.zeros_like(block_m...  746 us
    dynamic_slice x1024, local copies, waits for them, and re-layouts, column_step(): lax.dynamic_slice_in_dim(column, step_index, 1, 0)[0]  606 us
    reduce_scatter x1, waiting for transfers between devices, shards(): lax.psum_scatter(partial_sketch, ('wide', 'narrow'), scatter_dimension=0,...  151 us
    psum x1, waiting for transfers between devices, shards(): lax.psum((lax.dot_general(owned_rows, owned_rows, (((0,), (0,)), ((), ())...  92.9 us
    sub x1024, other arithmetic, column_step(): remaining = remaining - scaled[:, None] * scaled[None, :]  84.1 us
    dot_general x4, matrix products, add_block(): jnp.dot(one_hot, block_rows, precision=lax.Precision.HIGHEST, preferred_e...  69.3 us
    dot_general x140, matrix products, product(): jnp.dot(left, right, precision=lax.Precision.HIGHEST, preferred_element_t...  44.4 us

commit v1 on v0

v1 whole, which is shorter than its diff:
```python
import functools

import jax
import jax.numpy as jnp
from jax import lax
from jax.experimental import pallas as pl
from jax.experimental.pallas import tpu as pltpu
from jax.sharding import PartitionSpec as P

S = 2048
NB = 128
F32 = jnp.float32
BF = jnp.bfloat16

def split2(x):
    hi = x.astype(BF)
    lo = (x - hi.astype(F32)).astype(BF)
    return hi, lo

def dg(a, b, dims):
    return lax.dot_general(a, b, (dims, ((), ())), preferred_element_type=F32)

def dot3(a, b, dims=((1,), (0,))):
    ah, al = split2(a)
    bh, bl = split2(b)
    return dg(ah, bl, dims) + dg(al, bh, dims) + dg(ah, bh, dims)

def lane_bcast(x, c):
    return jnp.broadcast_to(x[:, c:c + 1], (8, NB))

def row_bcast(x, i):
    return jnp.broadcast_to(x[i:i + 1, :], (8, NB))

def gather_lanes(x, idx):
    return jnp.take_along_axis(x, idx, axis=1)

def diag_block(D, lane, sub):
    n = NB // 8
    A = list(D)
    T = [jnp.where(lane == sub + 8 * p, 1.0, 0.0).astype(F32) for p in range(n)]
    Rout, Tout = [], []
    for p in range(n):
        Ap, Tp = A[p], T[p]
        S = {}
        for k in range(8):
            bk = lane_bcast(Ap, 8 * p + k)
            for i in range(k, 8):
                S[i, k] = row_bcast(bk, i)
        rows = [row_bcast(Ap, i) for i in range(8)]
        trows = [row_bcast(Tp, i) for i in range(8)]
        for j in range(8):
            r = lax.rsqrt(S[j, j])
            rows[j] = rows[j] * r
            trows[j] = trows[j] * r
            ls = {}
            for i in range(j + 1, 8):
                ls[i] = S[i, j] * r
            for i in range(j + 1, 8):
                for k in range(j + 1, i + 1):
                    S[i, k] = S[i, k] - ls[i] * ls[k]
                rows[i] = rows[i] - ls[i] * rows[j]
                trows[i] = trows[i] - ls[i] * trows[j]
        Rp, Tpp = rows[0], trows[0]
        for j in range(1, 8):
            Rp = jnp.where(sub == j, rows[j], Rp)
            Tpp = jnp.where(sub == j, trows[j], Tpp)
        Rout.append(jnp.where(lane >= sub + 8 * p, Rp, 0.0))
        Tout.append(jnp.where(lane <= sub + 8 * p, Tpp, 0.0))
        for q in range(p + 1, n):
            idx = sub + 8 * q
            for j in range(8):
                c = gather_lanes(rows[j], idx)
                A[q] = A[q] - c * rows[j]
                T[q] = T[q] - c * trows[j]
    return Rout, Tout

def chol_kernel(nblk, share, idx_ref, g_ref, m_ref, r_out, y_out, x_out, a, t, m):
    W = nblk * NB
    lane = lax.broadcasted_iota(jnp.int32, (8, NB), 1)
    sub = lax.broadcasted_iota(jnp.int32, (8, NB), 0)
    a[...] = g_ref[...]
    m[...] = m_ref[...]

    def step(k, carry):
        o = pl.multiple_of(k * NB, NB)
        D = [a[pl.ds(pl.multiple_of(o + 8 * p, 8), 8), pl.ds(o, NB)] for p in range(NB // 8)]
        R, T = diag_block(D, lane, sub)
        for p in range(NB // 8):
            a[pl.ds(pl.multiple_of(o + 8 * p, 8), 8), pl.ds(o, NB)] = R[p]
            t[pl.ds(pl.multiple_of(o + 8 * p, 8), 8), :] = T[p]
        Tm = t[pl.ds(o, NB), :]
        yk = dot3(m[:, pl.ds(o, NB)], Tm, ((1,), (1,)))
        m[:, pl.ds(o, NB)] = yk
        for j in range(nblk):
            js = slice(j * NB, (j + 1) * NB)
            @pl.when(j < k)
            def _():
                a[pl.ds(o, NB), js] = jnp.zeros((NB, NB), F32)
            @pl.when(j > k)
            def _():
                rj = dot3(Tm, a[pl.ds(o, NB), js])
                a[pl.ds(o, NB), js] = rj
                m[:, js] = m[:, js] - dot3(yk, rj)
        for i in range(1, nblk):
            @pl.when(i > k)
            def _():
                is_ = slice(i * NB, (i + 1) * NB)
                rest = slice(i * NB, W)
                lhs = a[pl.ds(o, NB), is_]
                a[is_, rest] = a[is_, rest] - dot3(lhs, a[pl.ds(o, NB), rest], ((0,), (0,)))
        return carry
    lax.fori_loop(0, nblk, step, 0)
    y_out[...] = m[...]
    for k in range(nblk - 1, -1, -1):
        ks = slice(k * NB, (k + 1) * NB)
        xk = dot3(m[:, ks], t[ks, :])
        x_out[:, ks] = xk
        if k:
            m[:, :k * NB] = m[:, :k * NB] - dot3(xk, a[:k * NB, ks], ((1,), (1,)))
    r_out[...] = a[pl.ds(pl.multiple_of(idx_ref[0] * share, share), share), :]

def cholesky(gram, moments, index, share):
    W = gram.shape[0]
    nblk = W // NB
    vm = pl.BlockSpec(memory_space=pltpu.VMEM)
    return pl.pallas_call(
        functools.partial(chol_kernel, nblk, share),
        out_shape=(jax.ShapeDtypeStruct((share, W), F32),
                   jax.ShapeDtypeStruct(moments.shape, F32),
                   jax.ShapeDtypeStruct(moments.shape, F32)),
        in_specs=[pl.BlockSpec(memory_space=pltpu.SMEM), vm, vm],
        out_specs=(vm, vm, vm),
        scratch_shapes=[pltpu.VMEM((W, W), F32), pltpu.VMEM((W, NB), F32), pltpu.VMEM(moments.shape, F32)],
        compiler_params=pltpu.CompilerParams(vmem_limit_bytes=40 * 2**20),
        name="factor",
    )(index, gram, moments)


def shards(matrix, hashes, sign_bits, targets):
    rows_local = matrix.shape[0]
    width = matrix.shape[1]
    row_signs = (2 * sign_bits - 1).astype(jnp.float32)
    block = min(512, rows_local)
    block_count = rows_local // block
    bucket_range = lax.iota(jnp.int32, S)

    def add_block(block_index, running):
        offset = block_index * block
        bucket_ids = lax.dynamic_slice_in_dim(hashes, offset, block, 0)
        block_signs = lax.dynamic_slice_in_dim(row_signs, offset, block, 0)
        block_rows = lax.dynamic_slice_in_dim(matrix, offset, block, 0)
        one_hot = jnp.where(bucket_range[:, None] == bucket_ids[None, :], block_signs[None, :], 0.0)
        return running + jnp.dot(
            one_hot, block_rows, precision=lax.Precision.HIGHEST, preferred_element_type=jnp.float32
        )

    partial_sketch = lax.fori_loop(0, block_count, add_block, jnp.zeros((S, width), jnp.float32))
    moments_local = jnp.dot(
        targets, matrix, precision=lax.Precision.HIGHEST, preferred_element_type=jnp.float32
    )
    owned_rows = lax.psum_scatter(
        partial_sketch, ("wide", "narrow"), scatter_dimension=0, tiled=True
    )
    gram_matrix, moments = lax.psum(
        (
            lax.dot_general(
                owned_rows,
                owned_rows,
                (((0,), (0,)), ((), ())),
                precision=lax.Precision.HIGHEST,
                preferred_element_type=jnp.float32,
            ),
            moments_local,
        ),
        ("wide", "narrow"),
    )
    share = width // lax.axis_size("narrow")
    index = lax.axis_index("narrow").astype(jnp.int32).reshape(1)
    return cholesky(gram_matrix, moments, index, share)


def solution(mesh):
    return jax.shard_map(
        shards,
        mesh=mesh,
        in_specs=(
            P(("wide", "narrow"), None),
            P(("wide", "narrow")),
            P(("wide", "narrow")),
            P(None, ("wide", "narrow")),
        ),
        out_specs=(P("narrow", None), P(), P()),
        check_vma=False,
    )
```

time: 1960 us -> 441 us (0.23)
  loops' own time: 746 us -> 0.01 us
  local copies, waits for them, and re-layouts: 667 us -> 5.53 us
  other arithmetic: 104 us -> 0.71 us
  Pallas kernels: 0 us -> 55 us
  matrix products: 127 us -> 82.5 us
    another operation x8 -> x0, loops' own time: 746 us -> none  [factor_block(): lax.fori_loop(0, size, column_step, (block_matrix, jnp.zeros_like(block_m...]
    dynamic_slice x1025 -> x0, local copies, waits for them, and re-layouts: 607 us -> none  [the longest x1024 606 us: column_step(): lax.dynamic_slice_in_dim(column, step_index, 1, 0)[0]]
    sub x1024 -> x0, other arithmetic: 84.1 us -> none  [column_step(): remaining = remaining - scaled[:, None] * scaled[None, :]]
    pallas_call x0 -> x1, Pallas kernels: none -> 55 us  [cholesky(): pl.pallas_call(functools.partial(chol_kernel, nblk, share), out_shape=(ja...]
    dot_general x140 -> x0, matrix products: 44.4 us -> none  [product(): jnp.dot(left, right, precision=lax.Precision.HIGHEST, preferred_element_t...]
    dynamic_update_slice x1024 -> x0, local copies, waits for them, and re-layouts: 38.3 us -> none  [column_step(): lax.dynamic_update_slice_in_dim(lower_part, scaled[:, None], step_index, 1)]
where the time goes in v1:
time: 441 us
  waiting for transfers between devices  246 us (56%)
  matrix products  82.5 us (19%)
  Pallas kernels  55 us (12%)
  blocking collectives  37.5 us (9%)
  between operations  14.1 us (3%)
  local copies, waits for them, and re-layouts  5.53 us (1%)
    reduce_scatter x1, waiting for transfers between devices, shards(): lax.psum_scatter(partial_sketch, ('wide', 'narrow'), scatter_dimension=0,...  152 us
    psum x1, waiting for transfers between devices, shards(): lax.psum((lax.dot_general(owned_rows, owned_rows, (((0,), (0,)), ((), ())...  94 us
    dot_general x4, matrix products, add_block(): jnp.dot(one_hot, block_rows, precision=lax.Precision.HIGHEST, preferred_e...  69.1 us
    pallas_call x1, Pallas kernels, cholesky(): pl.pallas_call(functools.partial(chol_kernel, nblk, share), out_shape=(ja...  55 us
    psum x1, blocking collectives, shards(): lax.psum((lax.dot_general(owned_rows, owned_rows, (((0,), (0,)), ((), ())...  37.5 us
  transfers between devices with their start and end apart: 2, of which 2 were waited for; matrix products, arithmetic and copies ran while one was open for 2% of the time, Pallas kernels for 0%

profile of v1, /device:TPU:0, one launch (start us, length us, event | category | flops | bytes accessed | tf_op | source)
XLA Modules:
  0.0 440.9 jit_solution(16235267211911976722)
XLA Ops:
  7.2 0.0 copy-start
  7.2 0.0 reduce-scatter.2.cloned.1.call-start
  7.2 0.7 add_convert_fusion
  7.9 72.5 %while.14 = (s32[]{:T(128)}, f32[2048,1024]{1,0:T(8,128)}, s32[2048]{0:T(1024)}, f32[2048]{0:T(1024)S(1)}, f32[2048,1024]{1,0:T(8,128)}, /*index=5*/s32[]{:T(128)}, s32[]{:T(128)}, s32[]{:T(128)}, s32[]{:T(128)}) while((s32[]{:T(128)}, f32[2048,1024]{1,0:T(8,128)}, s32[2048]{0:T(1024)}, f32[2048]{0:T(1024)S(1)}, ...), condition=%wide.region_1.2_spmd.clone, body=%wide.region_0.1_spmd.clone.sunk | while | flops 12891193344 | bytes 18886816 | solution.py:157
  7.9 0.1 dynamic_slice.30
  8.0 0.8 dynamic_slice.31
  8.8 16.7 %select_add_fusion.2 = f32[2048,1024]{1,0:T(8,128)} fusion(f32[2048,1024]{1,0:T(8,128)} %get-tuple-element.184, pred[]{:T(512)S(6)} %compare.3, f32[2048,1024]{1,0:T(8,128)} %get-tuple-element.196, s32[]{:T(128)S(6)} %select_n.26, f32[512]{0:T(512)S(1)} %dynamic_slice.30, s32[512]{0:T(512)S(1)} %dynamic_slice.31), kind=kOutput, calls=%fused_computation.1.clone.1 | convolution fusion | flops 12891193344 | bytes 18878468 | tf_op jit(solution)/shard_map/while/body/eval_jaxpr/dot_general | solution.py:153
  25.5 0.1 dynamic_slice.30
  25.6 0.8 dynamic_slice.31
  26.3 17.5 %select_add_fusion.2 = f32[2048,1024]{1,0:T(8,128)} fusion(f32[2048,1024]{1,0:T(8,128)} %get-tuple-element.184, pred[]{:T(512)S(6)} %compare.3, f32[2048,1024]{1,0:T(8,128)} %get-tuple-element.196, s32[]{:T(128)S(6)} %select_n.26, f32[512]{0:T(512)S(1)} %dynamic_slice.30, s32[512]{0:T(512)S(1)} %dynamic_slice.31), kind=kOutput, calls=%fused_computation.1.clone.1 | convolution fusion | flops 12891193344 | bytes 18878468 | tf_op jit(solution)/shard_map/while/body/eval_jaxpr/dot_general | solution.py:153
  43.8 0.1 dynamic_slice.30
  43.9 0.8 dynamic_slice.31
  44.6 17.5 %select_add_fusion.2 = f32[2048,1024]{1,0:T(8,128)} fusion(f32[2048,1024]{1,0:T(8,128)} %get-tuple-element.184, pred[]{:T(512)S(6)} %compare.3, f32[2048,1024]{1,0:T(8,128)} %get-tuple-element.196, s32[]{:T(128)S(6)} %select_n.26, f32[512]{0:T(512)S(1)} %dynamic_slice.30, s32[512]{0:T(512)S(1)} %dynamic_slice.31), kind=kOutput, calls=%fused_computation.1.clone.1 | convolution fusion | flops 12891193344 | bytes 18878468 | tf_op jit(solution)/shard_map/while/body/eval_jaxpr/dot_general | solution.py:153
  62.1 0.1 dynamic_slice.30
  62.2 0.8 dynamic_slice.31
  62.9 17.5 %select_add_fusion.2 = f32[2048,1024]{1,0:T(8,128)} fusion(f32[2048,1024]{1,0:T(8,128)} %get-tuple-element.184, pred[]{:T(512)S(6)} %compare.3, f32[2048,1024]{1,0:T(8,128)} %get-tuple-element.196, s32[]{:T(128)S(6)} %select_n.26, f32[512]{0:T(512)S(1)} %dynamic_slice.30, s32[512]{0:T(512)S(1)} %dynamic_slice.31), kind=kOutput, calls=%fused_computation.1.clone.1 | convolution fusion | flops 12891193344 | bytes 18878468 | tf_op jit(solution)/shard_map/while/body/eval_jaxpr/dot_general | solution.py:153
  80.4 0.0 reduce-scatter.2.cloned.1.call-update
  80.4 0.0 all-reduce.2.cloned.1.call-start
  80.5 151.5 %reduce-scatter.2.cloned.1.call-done = f32[64,1024]{1,0:T(8,128)} async-done(((f32[2048,1024]{1,0:T(8,128)}), f32[64,1024]{1,0:T(8,128)}) %reduce-scatter.2.cloned.1.call-update) | async-done | bytes 262160 | tf_op jit(solution)/shard_map/reduce_scatter | solution.py:161
  232.0 6.4 %fusion.12 = f32[1024,1024]{1,0:T(8,128)} fusion(f32[64,1024]{1,0:T(8,128)} %reduce-scatter.2.cloned.1.call-done), kind=kOutput, calls=%fused_computation.12 | convolution fusion | flops 805306368 | bytes 4456448 | tf_op jit(solution)/shard_map/dot_general | solution.py:166
  238.4 0.0 all-reduce.2.cloned.1.call-update
  238.4 0.0 copy-done
  238.5 6.9 %fusion.13 = f32[8,1024]{1,0:T(8,128)S(1)} fusion(f32[8,2048]{1,0:T(8,128)S(1)} %copy-done, f32[2048,1024]{1,0:T(8,128)} %get-tuple-element.206), kind=kOutput, calls=%fused_computation.13 | convolution fusion | flops 201326592 | bytes 8486912 | tf_op jit(solution)/shard_map/dot_general | solution.py:158
  245.4 37.5 %psum.15.m_ref = f32[8,1024]{1,0:T(8,128)S(1)} all-reduce(f32[8,1024]{1,0:T(8,128)S(1)} %fusion.13), channel_id=1, replica_groups=mesh['wide'=8,'narrow'=4] {'wide','narrow'}, use_global_device_ids=true, to_apply=%region_4.5 | all-reduce | flops 8192 | bytes 65536 | tf_op jit(solution)/shard_map/psum | solution.py:164
  282.9 94.0 %all-reduce.2.cloned.1.call-done.g_ref = f32[1024,1024]{1,0:T(8,128)} async-done(((f32[1024,1024]{1,0:T(8,128)}), f32[1024,1024]{1,0:T(8,128)}) %all-reduce.2.cloned.1.call-update) | async-done | bytes 4194320 | tf_op jit(solution)/shard_map/psum | solution.py:164
  376.9 0.0 copy-start.1
  376.9 2.2 copy-done.1
  379.1 55.0 %factor.1 = (f32[256,1024]{1,0:T(8,128)}, f32[8,1024]{1,0:T(8,128)}, f32[8,1024]{1,0:T(8,128)}) custom-call(s32[1]{0:T(128)} %bitcast.idx_ref, f32[1024,1024]{1,0:T(8,128)S(1)} %copy-done.1, f32[8,1024]{1,0:T(8,128)S(1)} %psum.15.m_ref), custom_call_target="tpu_custom_call" | custom-call | tf_op jit(solution)/shard_map/factor/pallas_call | solution.py:126
  (1 shorter events, 0.0 us)
Async XLA Ops:
  7.2 231.3 %copy-start = (f32[8,2048]{1,0:T(8,128)S(1)}, f32[8,2048]{1,0:T(8,128)}, u32[]{:S(2)}) copy-start(f32[8,2048]{1,0:T(8,128)} %param.9) | copy-start | bytes 196612
  7.2 224.8 %reduce-scatter.2.cloned.1.call-start = ((), (), s32[]{:S(2)}) async-start(), calls=%async_computation.1 | async-start | bytes 8650752 | tf_op jit(solution)/shard_map/reduce_scatter | solution.py:161
  80.4 296.5 %all-reduce.2.cloned.1.call-start = ((), (), s32[]{:S(2)}) async-start(), calls=%async_computation.2 | async-start | bytes 8388608 | tf_op jit(solution)/shard_map/psum | solution.py:164
  376.9 2.2 copy-start.1
Sparse Core Ops, SparseCore 0:
  80.5 151.3 reduce-scatter.1
  238.6 138.2 all-reduce.1
